TPU v7x, 32 devices: a whole 2x2x4 slice. The times are simulated.
32 devices in a mesh: dp: 8 (over y, x, core), seq: 4 (over z).
Axes of the slice: x: 2, y: 2, z: 4, core: 2. Of those that a mesh axis runs over, the one named last changes fastest.
Arguments:
- tokens: bfloat16 [16, 1024, 1024], P('dp', 'seq'), may hold values from -17 to 17
- positions: int32 [16, 1024], P('dp', 'seq'), may hold values from 0 to 4092, as said below
- cotangent: bfloat16 [16, 1024, 1024], P('dp', 'seq'), may hold values from -6 to 6
- q_weight: bfloat16 [1024, 1024], P('dp'), may hold values from -0.1875 to 0.1875
- key_matrix: bfloat16 [1024, 512], P('dp'), may hold values from -0.1875 to 0.1875
- value_matrix: bfloat16 [1024, 512], P('dp'), may hold values from -0.1875 to 0.1875
- out_weight: bfloat16 [1024, 1024], P('dp'), may hold values from -2 to 2
- gate_weight: bfloat16 [1024, 4608], P('dp'), may hold values from -0.1875 to 0.1875
- up_weight: bfloat16 [1024, 4608], P('dp'), may hold values from -0.1875 to 0.1875
- down_weight: bfloat16 [1024, 4608], P('dp'), may hold values from -0.375 to 0.375
- attn_gain: float32 [1024], replicated, may hold values from 0.1 to 1.9
- ffn_gain: float32 [1024], replicated, may hold values from 0.1 to 1.9
- q_gain: float32 [64], replicated, may hold values from 0.1 to 1.9
- k_gain: float32 [64], replicated, may hold values from 0.1 to 1.9
Outputs:
- output: bfloat16 [16, 1024, 1024], P('dp', 'seq')
- input_grad: bfloat16 [16, 1024, 1024], P('dp', 'seq')
- q_weight_grad: float32 [1024, 1024], P('dp')
- k_weight_grad: float32 [1024, 512], P('dp')
- v_weight_grad: float32 [1024, 512], P('dp')
- out_weight_grad: float32 [1024, 1024], P('dp')
- gate_weight_grad: float32 [1024, 4608], P('dp')
- up_weight_grad: float32 [1024, 4608], P('dp')
- down_weight_grad: float32 [1024, 4608], P('dp')
- attn_gain_grad: float32 [1024], replicated
- ffn_gain_grad: float32 [1024], replicated
- q_gain_grad: float32 [64], replicated
- k_gain_grad: float32 [64], replicated
Inputs may be any that keep to these rules, and one draw needn't show every extreme that they name: Along each sequence the positions rise by 1 to 4 from one token to the next, the first being 0; in one sequence every step is 4.
All inputs are finite; a program needn't handle non-finite values.
Results may differ from a plain program's by a relative error of at most 0.02.
Values may be sent and summed in bfloat16 or wider, within the bound.
No kernel may reach another device: no remote copies, remote signals or barrier semaphores. Data moves between devices by JAX's collectives and lax.ppermute only.
A program may use at most 320 MiB of HBM per device.

v0:
```python
import jax
import jax.numpy as jnp
from jax import lax
from jax.sharding import PartitionSpec as P

epsilon = 1e-05
rope_base = 1000000.0
contract_last = (((1,), (1,)), ((), ()))
contract_first = (((0,), (0,)), ((), ()))


def rms_scale(value_heads):
    return lax.rsqrt(jnp.mean(value_heads * value_heads, axis=-1, keepdims=True) + epsilon)


def rotate(value_heads, cosines, sine_table):
    half_dim = value_heads.shape[-1] // 2
    first_half = value_heads[..., :half_dim]
    second_half = value_heads[..., half_dim:]
    return jnp.concatenate(
        [
            first_half * cosines - second_half * sine_table,
            second_half * cosines + first_half * sine_table,
        ],
        axis=-1,
    )


def unrotate(grads_in, cosines, sine_table):
    half_dim = grads_in.shape[-1] // 2
    first_half = grads_in[..., :half_dim]
    second_half = grads_in[..., half_dim:]
    return jnp.concatenate(
        [
            first_half * cosines + second_half * sine_table,
            second_half * cosines - first_half * sine_table,
        ],
        axis=-1,
    )


def angles(positions, head_dim):
    freq_index = jnp.arange(head_dim // 2, dtype=jnp.float32)
    inverse = rope_base ** (-(2.0 * freq_index) / head_dim)
    turned = positions.astype(jnp.float32)[:, None] * inverse[None, :]
    return (jnp.cos(turned)[:, None, :], jnp.sin(turned)[:, None, :])


def norm_back(grad_out, normed_hat, inv_scale, gain):
    scaled = grad_out * gain
    return inv_scale * (scaled - normed_hat * jnp.mean(scaled * normed_hat, axis=-1, keepdims=True))


def matmul(left, right):
    return jnp.dot(left, right, preferred_element_type=jnp.float32)


def matmul_t(left, right):
    return lax.dot_general(left, right, contract_last, preferred_element_type=jnp.float32)


def matmul_tn(left, right):
    return lax.dot_general(left, right, contract_first, preferred_element_type=jnp.float32)


def reduce_rows(term_fn, keep_rows):
    return lax.psum_scatter(
        term_fn(jnp.int32(0), lax.axis_size(("dp", "seq")) * keep_rows),
        ("dp", "seq"),
        scatter_dimension=0,
        tiled=True,
    )


def local(
    tokens,
    positions,
    cotangent,
    q_weight,
    key_matrix,
    value_matrix,
    out_weight,
    gate_weight,
    up_weight,
    down_weight,
    attn_gain,
    ffn_gain,
    q_gain,
    k_gain,
):
    seq_count, tok_local, model_width = tokens.shape
    rank_count = lax.axis_size("seq")
    row_count = seq_count * tok_local
    head_dim = q_gain.shape[0]
    q_cols = q_weight.shape[1]
    kv_cols = key_matrix.shape[1]
    ff_width = gate_weight.shape[1]
    local_q = q_cols // head_dim // rank_count
    local_kv = kv_cols // head_dim // rank_count
    group_size = local_q // local_kv
    sequence_length = tok_local * rank_count
    block_rows = min(512, sequence_length)
    block_count = sequence_length // block_rows
    score_scale = head_dim ** (-0.5)
    keep_rows = model_width // (lax.axis_size("dp") * rank_count)
    f32 = jnp.float32
    bf16 = jnp.bfloat16
    flat_in = tokens.reshape(row_count, model_width).astype(f32)
    in_scale = rms_scale(flat_in)
    in_hat = flat_in * in_scale
    normed_in = (in_hat * attn_gain).astype(bf16)
    q_part = lax.all_gather(q_weight, "dp", axis=0, tiled=True)
    k_part = lax.all_gather(key_matrix, "dp", axis=0, tiled=True)
    v_part = lax.all_gather(value_matrix, "dp", axis=0, tiled=True)
    out_part = lax.all_gather(out_weight, "dp", axis=0, tiled=True)
    columns = normed_in
    q_proj = matmul(columns, q_part)
    key_projected = matmul(columns, k_part)
    v_proj = matmul(columns, v_part)
    out_full = out_part
    cosines, sine_table = angles(positions.reshape(row_count), head_dim)
    q_heads = q_proj.reshape(row_count, q_cols // head_dim, head_dim)
    q_inv = rms_scale(q_heads)
    q_hat = q_heads * q_inv
    query_rows_all = rotate(q_hat * q_gain, cosines, sine_table).astype(bf16)
    key_heads = key_projected.reshape(row_count, kv_cols // head_dim, head_dim)
    k_inv = rms_scale(key_heads)
    k_hat = key_heads * k_inv
    key_rows = rotate(k_hat * k_gain, cosines, sine_table).astype(bf16)
    value_rows = v_proj.astype(bf16)
    q_send = query_rows_all.reshape(seq_count, tok_local, rank_count, local_q * head_dim)
    kv_send = jnp.concatenate(
        [
            key_rows.reshape(seq_count, tok_local, rank_count, local_kv * head_dim),
            value_rows.reshape(seq_count, tok_local, rank_count, local_kv * head_dim),
        ],
        axis=3,
    )
    q_here, kv_here = (
        lax.all_to_all(q_send, "seq", split_axis=2, concat_axis=1, tiled=True),
        lax.all_to_all(kv_send, "seq", split_axis=2, concat_axis=1, tiled=True),
    )
    q_local = q_here.reshape(seq_count, sequence_length, local_kv, group_size, head_dim)
    k_local = kv_here[:, :, 0, : local_kv * head_dim].reshape(
        seq_count, sequence_length, local_kv, head_dim
    )
    v_local = kv_here[:, :, 0, local_kv * head_dim :].reshape(
        seq_count, sequence_length, local_kv, head_dim
    )

    def block_scores(q_block, block_index):
        key_span = (block_index + 1) * block_rows
        raw_scores = (
            jnp.einsum(
                "sqhgd,skhd->shgqk", q_block, k_local[:, :key_span], preferred_element_type=f32
            )
            * score_scale
        )
        query_pos = block_index * block_rows + jnp.arange(block_rows)[:, None]
        key_pos = jnp.arange(key_span)[None, :]
        return jnp.where(key_pos <= query_pos, raw_scores, -1e30)

    attended_list = []
    log_list = []
    for block_index in range(block_count):
        row_lo = block_index * block_rows
        key_span = row_lo + block_rows
        scores = block_scores(q_local[:, row_lo : row_lo + block_rows], block_index)
        row_max = jnp.max(scores, axis=-1, keepdims=True)
        exp_terms = jnp.exp(scores - row_max)
        summed = jnp.sum(exp_terms, axis=-1, keepdims=True)
        probs = exp_terms / summed
        log_list.append(row_max + jnp.log(summed))
        attended_list.append(
            jnp.einsum(
                "shgqk,skhd->sqhgd",
                probs.astype(bf16),
                v_local[:, :key_span],
                preferred_element_type=f32,
            )
        )
    attended_output = jnp.concatenate(attended_list, axis=1)
    log_total = jnp.concatenate(log_list, axis=3)
    mixed_send = attended_output.astype(bf16).reshape(
        seq_count, sequence_length, 1, local_q * head_dim
    )
    mixed_back = lax.all_to_all(mixed_send, "seq", split_axis=1, concat_axis=2, tiled=True)
    mixed_rows = mixed_back.reshape(row_count, q_cols)
    residual = flat_in + matmul_t(mixed_rows, out_full)
    mid_scale = rms_scale(residual)
    mid_hat = residual * mid_scale
    normed_mid = (mid_hat * ffn_gain).astype(bf16)
    gate_part = lax.all_gather(gate_weight, "dp", axis=0, tiled=True)
    up_part = lax.all_gather(up_weight, "dp", axis=0, tiled=True)
    columns = normed_mid
    gate_proj = matmul(columns, gate_part)
    up_proj = matmul(columns, up_part)
    sigmoid_gate = jax.nn.sigmoid(gate_proj)
    activated = gate_proj * sigmoid_gate
    hidden = (activated * up_proj).astype(bf16)
    ffn_branch = matmul_t(hidden, lax.all_gather(down_weight, "dp", axis=0, tiled=True))
    output = (residual + ffn_branch).astype(bf16).reshape(seq_count, tok_local, model_width)
    d_ffn = cotangent.reshape(row_count, model_width)
    columns = d_ffn
    d_hidden = matmul(columns, lax.all_gather(down_weight, "dp", axis=0, tiled=True))
    d_gate = (d_hidden * up_proj * sigmoid_gate * (1.0 + gate_proj * (1.0 - sigmoid_gate))).astype(
        bf16
    )
    d_up = (d_hidden * activated).astype(bf16)
    gate_part, up_part = lax.all_gather((gate_weight, up_weight), "dp", axis=0, tiled=True)
    d_mid = matmul_t(d_gate, gate_part) + matmul_t(d_up, up_part)
    ffn_gain_part = jnp.sum(d_mid * mid_hat, axis=0)
    d_resid = d_ffn.astype(f32) + norm_back(d_mid, mid_hat, mid_scale, ffn_gain)
    d_attn = d_resid.astype(bf16)
    d_mixed = matmul(d_attn, out_full).astype(bf16)
    d_mixed_send = d_mixed.reshape(seq_count, tok_local, rank_count, local_q * head_dim)
    d_mixed_here = lax.all_to_all(d_mixed_send, "seq", split_axis=2, concat_axis=1, tiled=True)
    d_mixed_local = d_mixed_here.reshape(seq_count, sequence_length, local_kv, group_size, head_dim)
    d_key = jnp.zeros((seq_count, sequence_length, local_kv, head_dim), f32)
    d_value = jnp.zeros((seq_count, sequence_length, local_kv, head_dim), f32)
    d_query_list = []
    for block_index in range(block_count):
        row_lo = block_index * block_rows
        key_span = row_lo + block_rows
        q_block = q_local[:, row_lo : row_lo + block_rows]
        grad_block = d_mixed_local[:, row_lo : row_lo + block_rows]
        probs = jnp.exp(
            block_scores(q_block, block_index) - log_total[:, :, :, row_lo : row_lo + block_rows]
        )
        d_value = d_value.at[:, :key_span].add(
            jnp.einsum(
                "shgqk,sqhgd->skhd", probs.astype(bf16), grad_block, preferred_element_type=f32
            )
        )
        d_weights = jnp.einsum(
            "sqhgd,skhd->shgqk", grad_block, v_local[:, :key_span], preferred_element_type=f32
        )
        delta = jnp.sum(
            grad_block.astype(f32) * attended_output[:, row_lo : row_lo + block_rows], axis=-1
        )
        delta = jnp.transpose(delta, (0, 2, 3, 1))[..., None]
        d_scores = (probs * (d_weights - delta)).astype(bf16)
        d_query_list.append(
            jnp.einsum(
                "shgqk,skhd->sqhgd", d_scores, k_local[:, :key_span], preferred_element_type=f32
            )
            * score_scale
        )
        d_key = d_key.at[:, :key_span].add(
            jnp.einsum("shgqk,sqhgd->skhd", d_scores, q_block, preferred_element_type=f32)
            * score_scale
        )
    d_query = (
        jnp.concatenate(d_query_list, axis=1)
        .astype(bf16)
        .reshape(seq_count, sequence_length, 1, local_q * head_dim)
    )
    d_kv = jnp.concatenate(
        [
            d_key.astype(bf16).reshape(seq_count, sequence_length, 1, local_kv * head_dim),
            d_value.astype(bf16).reshape(seq_count, sequence_length, 1, local_kv * head_dim),
        ],
        axis=3,
    )
    d_query_rows, d_kv_rows = (
        lax.all_to_all(d_query, "seq", split_axis=1, concat_axis=2, tiled=True),
        lax.all_to_all(d_kv, "seq", split_axis=1, concat_axis=2, tiled=True),
    )
    d_q_rot = d_query_rows.reshape(row_count, q_cols // head_dim, head_dim).astype(f32)
    d_k_rot = (
        d_kv_rows[..., : local_kv * head_dim]
        .reshape(row_count, kv_cols // head_dim, head_dim)
        .astype(f32)
    )
    d_v_proj = d_kv_rows[..., local_kv * head_dim :].reshape(row_count, kv_cols)
    d_q_normed = unrotate(d_q_rot, cosines, sine_table)
    d_k_normed = unrotate(d_k_rot, cosines, sine_table)
    q_gain_part = jnp.sum(d_q_normed * q_hat, axis=(0, 1))
    k_gain_part = jnp.sum(d_k_normed * k_hat, axis=(0, 1))
    d_q_proj = norm_back(d_q_normed, q_hat, q_inv, q_gain).reshape(row_count, q_cols).astype(bf16)
    d_k_proj = norm_back(d_k_normed, k_hat, k_inv, k_gain).reshape(row_count, kv_cols).astype(bf16)
    q_part, k_part, v_part = lax.all_gather(
        (q_weight, key_matrix, value_matrix), "dp", axis=0, tiled=True
    )
    d_normed_in = (
        matmul_t(d_q_proj, q_part) + matmul_t(d_k_proj, k_part) + matmul_t(d_v_proj, v_part)
    )
    attn_gain_part = jnp.sum(d_normed_in * in_hat, axis=0)
    input_grad = (
        (d_resid + norm_back(d_normed_in, in_hat, in_scale, attn_gain))
        .astype(bf16)
        .reshape(seq_count, tok_local, model_width)
    )

    def every_term(offset, amount):
        return jnp.concatenate(
            [
                jnp.concatenate(
                    [
                        matmul_tn(normed_mid, d_gate),
                        matmul_tn(normed_mid, d_up),
                        matmul_tn(d_ffn, hidden),
                    ],
                    axis=1,
                ),
                matmul_tn(d_attn, mixed_rows),
                jnp.concatenate(
                    [
                        matmul_tn(normed_in, d_q_proj),
                        matmul_tn(normed_in, d_k_proj),
                        matmul_tn(normed_in, d_v_proj),
                    ],
                    axis=1,
                ),
            ],
            axis=1,
        )

    combined = reduce_rows(every_term, keep_rows)
    ffn_part = combined[:, : 3 * ff_width]
    out_part = combined[:, 3 * ff_width : 3 * ff_width + q_cols]
    first_part = combined[:, 3 * ff_width + q_cols :]
    ffn_full, out_grad, first_full = (
        lax.all_gather(ffn_part.astype(jnp.bfloat16), "seq", axis=0, tiled=True).astype(
            ffn_part.dtype
        ),
        lax.all_gather(out_part.astype(jnp.bfloat16), "seq", axis=0, tiled=True).astype(
            out_part.dtype
        ),
        lax.all_gather(first_part.astype(jnp.bfloat16), "seq", axis=0, tiled=True).astype(
            first_part.dtype
        ),
    )
    gain_grads = lax.psum((attn_gain_part, ffn_gain_part, q_gain_part, k_gain_part), ("dp", "seq"))
    return (
        output,
        input_grad,
        first_full[:, :q_cols],
        first_full[:, q_cols : q_cols + kv_cols],
        first_full[:, q_cols + kv_cols :],
        out_grad,
        ffn_full[:, :ff_width],
        ffn_full[:, ff_width : 2 * ff_width],
        ffn_full[:, 2 * ff_width :],
        gain_grads[0],
        gain_grads[1],
        gain_grads[2],
        gain_grads[3],
    )


def solution(mesh):
    in_specs = (
        P("dp", "seq", None),
        P("dp", "seq"),
        P("dp", "seq", None),
        P("dp", None),
        P("dp", None),
        P("dp", None),
        P("dp", None),
        P("dp", None),
        P("dp", None),
        P("dp", None),
        P(),
        P(),
        P(),
        P(),
    )
    out_specs = (
        P("dp", "seq", None),
        P("dp", "seq", None),
        P("dp", None),
        P("dp", None),
        P("dp", None),
        P("dp", None),
        P("dp", None),
        P("dp", None),
        P("dp", None),
        P(),
        P(),
        P(),
        P(),
    )
    return jax.shard_map(local, mesh=mesh, in_specs=in_specs, out_specs=out_specs, check_vma=False)
```

profile of v0, /device:TPU:0, one launch (start us, length us, event | category | flops | bytes accessed | tf_op | source)
XLA Modules:
  0.0 1240.2 jit_solution(9845809243946968209)
XLA Ops:
  13.9 22.2 %all-gather.11.cloned.1.call-done = bf16[1024,512]{1,0:T(8,128)(2,1)} async-done(((bf16[128,512]{1,0:T(8,128)(2,1)}), bf16[1024,512]{1,0:T(8,128)(2,1)}) %all-gather.11.cloned.1.call-update) | async-done | bytes 1048592 | tf_op jit(solution)/shard_map/all_gather | solution.py:114
  40.9 20.6 %all-gather.9.cloned.1.call-done = bf16[1024,512]{1,0:T(8,128)(2,1)} async-done(((bf16[128,512]{1,0:T(8,128)(2,1)}), bf16[1024,512]{1,0:T(8,128)(2,1)}) %all-gather.9.cloned.1.call-update) | async-done | bytes 1048592 | tf_op jit(solution)/shard_map/all_gather | solution.py:113
  68.0 4.6 all-to-all-start
  72.6 18.8 %all-gather.13.cloned.1.call-done = bf16[1024,1024]{1,0:T(8,128)(2,1)} async-done(((bf16[128,1024]{1,0:T(8,128)(2,1)}), bf16[1024,1024]{1,0:T(8,128)(2,1)}) %all-gather.13.cloned.1.call-update) | async-done | bytes 2097168 | tf_op jit(solution)/shard_map/all_gather | solution.py:112
  91.4 3.9 copy.109
  101.6 4.8 all-to-all-start.1
  109.9 22.6 %all-to-all-done.1 = bf16[2,256,4,256]{1,0,3,2:T(2,128)(2,1)S(1)} async-done(((bf16[2,256,4,256]{1,0,3,2:T(2,128)(2,1)}), bf16[2,256,4,256]{1,0,3,2:T(2,128)(2,1)S(1)}, u32[]{:S(2)}, u32[]{:S(2)}) %all-to-all-start.1) | async-done | bytes 1048608 | tf_op jit(solution)/shard_map/all_to_all | solution.py:140
  138.6 3.3 fusion.85
  143.9 7.5 fusion.5
  151.5 10.7 fusion.2
  162.2 9.4 fusion.84
  174.4 3.9 all-to-all-start.2
  178.3 25.2 %all-to-all-done.2 = bf16[2,1024,1,256]{3,0,2,1:T(2,128)(2,1)S(1)} async-done(((bf16[2,1024,1,256]{3,0,2,1:T(2,128)(2,1)}), bf16[2,1024,1,256]{3,0,2,1:T(2,128)(2,1)S(1)}, u32[]{:S(2)}, u32[]{:S(2)}) %all-to-all-start.2) | async-done | bytes 1048608 | tf_op jit(solution)/shard_map/all_to_all | solution.py:187
  205.8 3.3 multiply_reduce_fusion.4
  209.4 12.1 fusion.87
  221.4 20.8 %all-gather.17.cloned.1.call-done = bf16[1024,4608]{1,0:T(8,128)(2,1)} async-done(((bf16[128,4608]{1,0:T(8,128)(2,1)}), bf16[1024,4608]{1,0:T(8,128)(2,1)}) %all-gather.17.cloned.1.call-update) | async-done | bytes 9437200 | tf_op jit(solution)/shard_map/all_gather | solution.py:193
  242.3 11.0 fusion.86
  253.3 49.7 %all-gather.21.cloned.1.call-done = bf16[1024,4608]{1,0:T(8,128)(2,1)} async-done(((bf16[128,4608]{1,0:T(8,128)(2,1)}), bf16[1024,4608]{1,0:T(8,128)(2,1)}) %all-gather.21.cloned.1.call-update) | async-done | bytes 9437200 | tf_op jit(solution)/shard_map/all_gather | solution.py:201
  303.0 17.6 %multiply_convert_fusion = (bf16[512,4608]{1,0:T(8,128)(2,1)}, bf16[512,4608]{1,0:T(8,128)(2,1)}, bf16[512,4608]{1,0:T(8,128)(2,1)}) fusion(f32[512,4608]{1,0:T(8,128)} %fusion.86, f32[512,4608]{1,0:T(8,128)} %fusion.87, bf16[512,1024]{1,0:T(8,128)(2,1)} %bitcast.306, bf16[1024,4608]{1,0:T(8,128)(2,1)} %all-gather.21.cloned.1.call-done), kind=kOutput, calls=%fused_computation.12 | convolution fusion | flops 4867227648 | bytes 43515904 | tf_op jit(solution)/shard_map/dot_general | solution.py:55
  320.6 9.2 fusion.88
  329.8 8.1 multiply_reduce_fusion.1
  347.6 4.8 all-to-all-start.3
  352.4 11.8 convolution_dynamic-update-slice_fusion.1
  364.1 11.6 convolution_dynamic-update-slice_fusion
  383.5 5.9 fusion.50
  389.9 6.4 fusion.7
  396.3 8.9 fusion.44
  405.1 11.2 fusion.1
  418.3 3.6 fusion.54
  421.9 6.8 fusion.47
  430.0 3.1 pad_maximum_fusion.5
  433.2 4.2 all-to-all-start.5
  437.4 11.8 bitcast_dynamic-update-slice_fusion
  449.3 4.9 fusion.49
  455.3 4.0 fusion.48
  461.2 3.5 pad_maximum_fusion.4
  464.8 5.0 all-to-all-start.4
  470.2 3.4 convolution_dynamic-update-slice_fusion.3
  485.6 9.0 all-to-all-done.4
  497.5 4.2 copy.124
  501.7 3.9 reshape.510
  509.4 3.4 convolution_dynamic-update-slice_fusion.2
  517.4 612.6 %reduce-scatter.2.cloned.1.call-done = f32[32,16896]{1,0:T(8,128)} async-done(((f32[1024,16896]{1,0:T(8,128)}), f32[32,16896]{1,0:T(8,128)}) %reduce-scatter.2.cloned.1.call-update) | async-done | bytes 2162704 | tf_op jit(solution)/shard_map/reduce_scatter | solution.py:67
  1133.7 10.3 add_convert_fusion
  1148.9 42.6 %all-reduce.2 = (f32[1024]{0:T(1024)}, f32[1024]{0:T(1024)}, f32[64]{0:T(128)}, f32[64]{0:T(128)}) all-reduce(f32[1024]{0:T(1024)S(1)} %get-tuple-element.81, f32[1024]{0:T(1024)S(1)} %get-tuple-element.79, f32[64]{0:T(128)S(1)} %get-tuple-element.77, f32[64]{0:T(128)S(1)} %get-tuple-element.83), channel_id=1, replica_groups=mesh['dp'=8,'seq'=4] {'dp','seq'}, use_global_device_ids=true, to_apply=%region_16.17 | all-reduce | flops 2176 | bytes 17408 | tf_op jit(solution)/shard_map/psum | solution.py:334
  1194.7 15.7 %all_gather.44 = bf16[128,1024]{1,0:T(8,128)(2,1)S(1)} all-gather(bf16[32,1024]{1,0:T(8,128)(2,1)S(1)} %slice-done), channel_id=1, replica_groups=mesh['dp'=8,'seq'=4] {'seq'}, dimensions={0}, use_global_device_ids=true | all-gather | bytes 327680 | tf_op jit(solution)/shard_map/all_gather | solution.py:327
  1211.2 15.4 %all_gather.43 = bf16[128,2048]{1,0:T(8,128)(2,1)S(1)} all-gather(bf16[32,2048]{1,0:T(8,128)(2,1)S(1)} %slice-done.1), channel_id=1, replica_groups=mesh['dp'=8,'seq'=4] {'seq'}, dimensions={0}, use_global_device_ids=true | all-gather | bytes 655360 | tf_op jit(solution)/shard_map/all_gather | solution.py:330
  1228.3 5.2 fusion.80
  (221 shorter events, 102.5 us)
Async XLA Ops:
  7.2 5.7 copy-start.43
  7.2 28.9 %all-gather.11.cloned.1.call-start = ((), (), s32[]{:S(2)}) async-start(), calls=%async_computation.8 | async-start | bytes 1179648 | tf_op jit(solution)/shard_map/all_gather | solution.py:114
  7.9 53.6 %all-gather.9.cloned.1.call-start = ((), (), s32[]{:S(2)}) async-start(), calls=%async_computation.7 | async-start | bytes 1179648 | tf_op jit(solution)/shard_map/all_gather | solution.py:113
  8.7 82.7 %all-gather.13.cloned.1.call-start = ((), (), s32[]{:S(2)}) async-start(), calls=%async_computation.9 | async-start | bytes 2359296 | tf_op jit(solution)/shard_map/all_gather | solution.py:112
  9.4 196.3 %all-gather.15.cloned.1.call-start = ((), (), s32[]{:S(2)}) async-start(), calls=%async_computation.10 | async-start | bytes 2359296 | tf_op jit(solution)/shard_map/all_gather | solution.py:115
  10.0 199.4 %all-gather.19.cloned.1.call-start = ((), (), s32[]{:S(2)}) async-start(), calls=%async_computation.12 | async-start | bytes 10616832 | tf_op jit(solution)/shard_map/all_gather | solution.py:194
  10.6 231.7 %all-gather.17.cloned.1.call-start = ((), (), s32[]{:S(2)}) async-start(), calls=%async_computation.11 | async-start | bytes 10616832 | tf_op jit(solution)/shard_map/all_gather | solution.py:193
  11.2 291.8 %all-gather.21.cloned.1.call-start = ((), (), s32[]{:S(2)}) async-start(), calls=%async_computation.13 | async-start | bytes 10616832 | tf_op jit(solution)/shard_map/all_gather | solution.py:201
  13.3 82.1 %copy-start.11 = (bf16[2,256,1024]{2,1,0:T(8,128)(2,1)}, bf16[2,256,1024]{2,1,0:T(8,128)(2,1)S(1)}, u32[]{:S(2)}) copy-start(bf16[2,256,1024]{2,1,0:T(8,128)(2,1)S(1)} %fusion.32) | copy-start | bytes 3145732
  13.9 86.1 %copy-start.26 = (f32[512,32]{0,1:T(8,128)}, f32[512,32]{0,1:T(8,128)S(1)}, u32[]{:S(2)}) copy-start(f32[512,32]{0,1:T(8,128)S(1)} %get-tuple-element.111) | copy-start | bytes 196612
  13.9 86.1 %copy-start.28 = (f32[512,32]{0,1:T(8,128)}, f32[512,32]{0,1:T(8,128)S(1)}, u32[]{:S(2)}) copy-start(f32[512,32]{0,1:T(8,128)S(1)} %get-tuple-element.112) | copy-start | bytes 196612
  38.9 25.9 %copy-start.50 = (f32[64]{0:T(128)S(1)}, f32[64]{0:T(128)}, u32[]{:S(2)}) copy-start(f32[64]{0:T(128)} %param.39) | copy-start | bytes 772
  68.0 33.6 %all-to-all-start = ((bf16[2,256,4,256]{3,1,0,2:T(8,128)(2,1)}), bf16[2,256,4,256]{3,1,0,2:T(8,128)(2,1)S(1)}, u32[]{:S(2)}, u32[]{:S(2)}) async-start(bf16[2,256,4,256]{3,1,0,2:T(8,128)(2,1)} %pad_maximum_fusion.1), calls=%async_computation | async-start | bytes 2097152 | tf_op jit(solution)/shard_map/all_to_all | solution.py:141
  91.4 8.2 copy-start.48
  101.6 30.9 %all-to-all-start.1 = ((bf16[2,256,4,256]{1,0,3,2:T(2,128)(2,1)}), bf16[2,256,4,256]{1,0,3,2:T(2,128)(2,1)S(1)}, u32[]{:S(2)}, u32[]{:S(2)}) async-start(bf16[2,256,4,256]{1,0,3,2:T(2,128)(2,1)} %convert_element_type.176), calls=%async_computation.1 | async-start | bytes 2097152 | tf_op jit(solution)/shard_map/all_to_all | solution.py:140
  134.1 9.8 copy-start.14
  151.4 10.7 copy-start.39
  162.2 9.8 copy-start.25
  174.4 29.2 %all-to-all-start.2 = ((bf16[2,1024,1,256]{3,0,2,1:T(2,128)(2,1)}), bf16[2,1024,1,256]{3,0,2,1:T(2,128)(2,1)S(1)}, u32[]{:S(2)}, u32[]{:S(2)}) async-start(bf16[2,1024,1,256]{3,0,2,1:T(2,128)(2,1)} %pad_maximum_fusion.3), calls=%async_computation.2 | async-start | bytes 2097152 | tf_op jit(solution)/shard_map/all_to_all | solution.py:187
  209.1 120.7 %copy-start.7 = (f32[512,1024]{1,0:T(8,128)}, f32[512,1024]{1,0:T(8,128)S(1)}, u32[]{:S(2)}) copy-start(f32[512,1024]{1,0:T(8,128)S(1)} %get-tuple-element.128) | copy-start | bytes 6291460
  320.6 9.2 copy-start.9
  329.8 8.1 copy-start.33
  347.6 31.0 %all-to-all-start.3 = ((bf16[2,256,4,256]{1,3,0,2:T(8,128)(2,1)}), bf16[2,256,4,256]{1,3,0,2:T(8,128)(2,1)}, u32[]{:S(2)}, u32[]{:S(2)}) async-start(bf16[2,256,4,256]{1,3,0,2:T(8,128)(2,1)} %copy.117), calls=%async_computation.3 | async-start | bytes 2097152 | tf_op jit(solution)/shard_map/all_to_all | solution.py:217
  383.4 12.9 %copy-start.17 = (bf16[2,1024,2,2,64]{1,4,3,2,0:T(8,128)(2,1)}, bf16[2,1024,2,2,64]{1,4,3,2,0:T(8,128)(2,1)S(1)}, u32[]{:S(2)}) copy-start(bf16[2,1024,2,2,64]{1,4,3,2,0:T(8,128)(2,1)S(1)} %reshape.504) | copy-start | bytes 3145732
  383.4 6.0 copy-start.31
  383.4 6.0 copy-start.32
  383.4 6.4 copy-start.40
  389.9 6.4 copy-start.21
  405.1 13.2 %copy-start.15 = (bf16[2,1024,2,2,64]{1,4,3,2,0:T(8,128)(2,1)S(1)}, bf16[2,1024,2,2,64]{1,4,3,2,0:T(8,128)(2,1)}, u32[]{:S(2)}) copy-start(bf16[2,1024,2,2,64]{1,4,3,2,0:T(8,128)(2,1)} %copy-done.14) | copy-start | bytes 3145732
  433.2 31.6 %all-to-all-start.5 = ((bf16[2,1024,1,256]{3,0,2,1:T(2,128)(2,1)}), bf16[2,1024,1,256]{3,0,2,1:T(2,128)(2,1)}, u32[]{:S(2)}, u32[]{:S(2)}) async-start(bf16[2,1024,1,256]{3,0,2,1:T(2,128)(2,1)} %pad_maximum_fusion.5), calls=%async_computation.5 | async-start | bytes 2097152 | tf_op jit(solution)/shard_map/all_to_all | solution.py:267
  437.4 11.9 copy-start.19
  455.3 14.9 %copy-start.16 = (bf16[64,8,4,256]{3,1,2,0:T(8,128)(2,1)S(1)}, bf16[64,8,4,256]{3,1,2,0:T(8,128)(2,1)}, u32[]{:S(2)}) copy-start(bf16[64,8,4,256]{3,1,2,0:T(8,128)(2,1)} %copy.162) | copy-start | bytes 3145732
  464.8 29.9 %all-to-all-start.4 = ((bf16[2,1024,1,256]{3,0,2,1:T(2,128)(2,1)}), bf16[2,1024,1,256]{3,0,2,1:T(2,128)(2,1)}, u32[]{:S(2)}, u32[]{:S(2)}) async-start(bf16[2,1024,1,256]{3,0,2,1:T(2,128)(2,1)} %pad_maximum_fusion.4), calls=%async_computation.4 | async-start | bytes 2097152 | tf_op jit(solution)/shard_map/all_to_all | solution.py:266
  469.8 660.2 %reduce-scatter.2.cloned.1.call-start = ((), (), s32[]{:S(2)}) async-start(), calls=%async_computation.14 | async-start | bytes 71368704 | tf_op jit(solution)/shard_map/reduce_scatter | solution.py:67
  473.7 9.1 copy-start.27
  473.7 9.1 copy-start.29
  475.1 9.0 copy-start.5
  475.1 9.0 copy-start.42
  475.1 9.0 copy-start.51
  501.7 5.9 copy-start.37
  501.7 5.9 copy-start.49
  509.4 5.7 copy-start.34
  517.2 711.1 %all-gather.23.cloned.1.call-start = ((), (), s32[]{:S(2)}) async-start(), calls=%async_computation.15 | async-start | bytes 4423680 | tf_op jit(solution)/shard_map/all_gather | solution.py:324
  1133.7 10.3 copy-start.13
  1133.7 11.1 copy-start.24
  1133.7 11.1 copy-start.35
  1148.9 45.7 %slice-start = ((bf16[32,16896]{1,0:T(8,128)(2,1)}), bf16[32,1024]{1,0:T(8,128)(2,1)S(1)}, s32[]{:S(2)}) async-start(bf16[32,16896]{1,0:T(8,128)(2,1)} %copy-done.10), calls=%async_computation.16 | async-start | bytes 131072 | tf_op jit(solution)/shard_map/slice | solution.py:321
  1148.9 62.3 %slice-start.1 = ((bf16[32,16896]{1,0:T(8,128)(2,1)}), bf16[32,2048]{1,0:T(8,128)(2,1)S(1)}, s32[]{:S(2)}) async-start(bf16[32,16896]{1,0:T(8,128)(2,1)} %copy-done.10), calls=%async_computation.17 | async-start | bytes 262144 | tf_op jit(solution)/shard_map/slice | solution.py:322
  (22 other events, 56.8 us)
Sparse Core Ops, SparseCore 0:
  9.9 26.1 all-gather.10
  38.0 23.4 all-gather.8
  63.5 27.8 all-gather.12
  93.1 27.8 all-gather.14
  122.8 58.8 all-gather.18
  183.4 58.8 all-gather.16
  244.1 58.8 all-gather.20
  517.3 612.6 reduce-scatter.1
  1133.8 73.3 all-gather.22
where the time goes:
time: 1250 us; the launch traced here: 1240 us
  waiting for transfers between devices  809 us (65%)
  matrix products  206 us (16%)
  blocking collectives  73.7 us (6%)
  local copies, waits for them, and re-layouts  63 us (5%)
  other arithmetic  45.8 us (4%)
  starting transfers between devices  28.2 us (2%)
  between operations  15 us (1%)
    reduce_scatter x1, waiting for transfers between devices, reduce_rows(): lax.psum_scatter(term_fn(jnp.int32(0), lax.axis_size(('dp', 'seq')) * kee...  613 us
    all_gather x1, waiting for transfers between devices, local(): lax.all_gather(down_weight, 'dp', axis=0, tiled=True)  49.7 us
    dot_general x7, matrix products, matmul(): return jnp.dot(left, right, preferred_element_type=jnp.float32)  49.3 us
    dot_general x7, matrix products, matmul_tn(): lax.dot_general(left, right, contract_first, preferred_element_type=jnp.f...  46.4 us
    psum x1, blocking collectives, local(): lax.psum((attn_gain_part, ffn_gain_part, q_gain_part, k_gain_part), ('dp'...  42.6 us
    dot_general x7, matrix products, matmul_t(): lax.dot_general(left, right, contract_last, preferred_element_type=jnp.fl...  35.4 us
    all_to_all x1, waiting for transfers between devices, local(): lax.all_to_all(mixed_send, 'seq', split_axis=1, concat_axis=2, tiled=True)  25.2 us
  transfers between devices with their start and end apart: 15, of which 10 were waited for; matrix products, arithmetic and copies ran while one was open for 15% of the time, Pallas kernels for 0%

commit v1 on v0

--- a/solution.py
+++ b/solution.py
@@ -2,6 +2,7 @@
 import jax.numpy as jnp
 from jax import lax
 from jax.sharding import PartitionSpec as P
+from jax.lax import axis_index, axis_size, ppermute
 
 epsilon = 1e-05
 rope_base = 1000000.0
@@ -198,7 +199,20 @@
     sigmoid_gate = jax.nn.sigmoid(gate_proj)
     activated = gate_proj * sigmoid_gate
     hidden = (activated * up_proj).astype(bf16)
-    ffn_branch = matmul_t(hidden, lax.all_gather(down_weight, "dp", axis=0, tiled=True))
+
+    def save_records(raw, axis_key):
+        amount_of = axis_size(axis_key)
+        panels = list(map(lambda to_i: (to_i, (to_i + 1) % amount_of), range(amount_of)))
+        history = list(map(lambda to_i: (to_i, (to_i - 1) % amount_of), range(amount_of)))
+        moved, n_now = ([raw], [raw])
+        for _ in range(amount_of // 2):
+            moved.append(ppermute(moved[-1], axis_key, perm=panels))
+        for _ in range((amount_of - 1) // 2):
+            n_now.append(ppermute(n_now[-1], axis_key, perm=history))
+        high = jnp.concatenate([*moved[::-1], *n_now[1:]], axis=0)
+        return jnp.roll(high, (axis_index(axis_key) - amount_of // 2) * raw.shape[0], axis=0)
+
+    ffn_branch = matmul_t(hidden, save_records(down_weight, "dp"))
     output = (residual + ffn_branch).astype(bf16).reshape(seq_count, tok_local, model_width)
     d_ffn = cotangent.reshape(row_count, model_width)
     columns = d_ffn

time: 1250 us -> 1260 us (level)
  waiting for transfers between devices: 809 us -> 771 us
  local copies, waits for them, and re-layouts: 63 us -> 94.5 us
  starting transfers between devices: 28.2 us -> 47 us
    reduce_scatter x1, waiting for transfers between devices: 613 us -> 489 us  [reduce_rows(): lax.psum_scatter(term_fn(jnp.int32(0), lax.axis_size(('dp', 'seq')) * kee...]
    ppermute x0 -> x7, waiting for transfers between devices: none -> 95.1 us  [the longest x4 95.1 us: save_records(): moved.append(ppermute(moved[-1], axis_key, perm=panels))]
    unnamed x109 -> x146, local copies, waits for them, and re-layouts: 5.2 us -> 35.6 us
  transfers between devices with their start and end apart: 15 -> 22, of which waited for: 10 -> 14; matrix products, arithmetic and copies ran while one was open for 15% -> 17% of each run, Pallas kernels for 0% -> 0%
where the time goes in v1:
time: 1260 us; the launch traced here: 1250 us
  waiting for transfers between devices  771 us (61%)
  matrix products  206 us (16%)
  local copies, waits for them, and re-layouts  94.5 us (8%)
  blocking collectives  73.2 us (6%)
  starting transfers between devices  47 us (4%)
  other arithmetic  43.9 us (3%)
  between operations  15.3 us (1%)
    reduce_scatter x1, waiting for transfers between devices, reduce_rows(): lax.psum_scatter(term_fn(jnp.int32(0), lax.axis_size(('dp', 'seq')) * kee...  489 us
    ppermute x4, waiting for transfers between devices, save_records(): moved.append(ppermute(moved[-1], axis_key, perm=panels))  95.1 us
    all_gather x1, waiting for transfers between devices, local(): lax.all_gather(down_weight, 'dp', axis=0, tiled=True)  49.6 us
    dot_general x7, matrix products, matmul(): return jnp.dot(left, right, preferred_element_type=jnp.float32)  47.9 us
    dot_general x7, matrix products, matmul_tn(): lax.dot_general(left, right, contract_first, preferred_element_type=jnp.f...  46.4 us
    psum x1, blocking collectives, local(): lax.psum((attn_gain_part, ffn_gain_part, q_gain_part, k_gain_part), ('dp'...  44 us
    dot_general x7, matrix products, matmul_t(): lax.dot_general(left, right, contract_last, preferred_element_type=jnp.fl...  37.1 us
    unnamed x146, local copies, waits for them, and re-layouts  35.6 us
  transfers between devices with their start and end apart: 22, of which 14 were waited for; matrix products, arithmetic and copies ran while one was open for 17% of the time, Pallas kernels for 0%

profile of v1, /device:TPU:0, one launch (start us, length us, event | category | flops | bytes accessed | tf_op | source)
XLA Modules:
  0.0 1250.4 jit_solution(2866516812777532229)
XLA Ops:
  13.9 22.2 %all-gather.11.cloned.1.call-done = bf16[1024,512]{1,0:T(8,128)(2,1)} async-done(((bf16[128,512]{1,0:T(8,128)(2,1)}), bf16[1024,512]{1,0:T(8,128)(2,1)}) %all-gather.11.cloned.1.call-update) | async-done | bytes 1048592 | tf_op jit(solution)/shard_map/all_gather | solution.py:115
  40.9 20.6 %all-gather.9.cloned.1.call-done = bf16[1024,512]{1,0:T(8,128)(2,1)} async-done(((bf16[128,512]{1,0:T(8,128)(2,1)}), bf16[1024,512]{1,0:T(8,128)(2,1)}) %all-gather.9.cloned.1.call-update) | async-done | bytes 1048592 | tf_op jit(solution)/shard_map/all_gather | solution.py:114
  68.0 4.6 all-to-all-start
  72.6 18.8 %all-gather.13.cloned.1.call-done = bf16[1024,1024]{1,0:T(8,128)(2,1)} async-done(((bf16[128,1024]{1,0:T(8,128)(2,1)}), bf16[1024,1024]{1,0:T(8,128)(2,1)}) %all-gather.13.cloned.1.call-update) | async-done | bytes 2097168 | tf_op jit(solution)/shard_map/all_gather | solution.py:113
  91.4 3.9 copy.109
  101.6 4.8 all-to-all-start.1
  110.0 22.6 %all-to-all-done.1 = bf16[2,256,4,256]{1,0,3,2:T(2,128)(2,1)S(1)} async-done(((bf16[2,256,4,256]{1,0,3,2:T(2,128)(2,1)}), bf16[2,256,4,256]{1,0,3,2:T(2,128)(2,1)S(1)}, u32[]{:S(2)}, u32[]{:S(2)}) %all-to-all-start.1) | async-done | bytes 1048608 | tf_op jit(solution)/shard_map/all_to_all | solution.py:141
  143.9 7.6 fusion.7
  151.6 10.6 fusion.2
  162.2 9.4 fusion.89
  174.4 14.6 %all-to-all-start.2 = ((bf16[2,1024,1,256]{3,0,2,1:T(2,128)(2,1)}), bf16[2,1024,1,256]{3,0,2,1:T(2,128)(2,1)S(1)}, u32[]{:S(2)}, u32[]{:S(2)}) async-start(bf16[2,1024,1,256]{3,0,2,1:T(2,128)(2,1)} %pad_maximum_fusion.3), calls=%async_computation.2 | async-start | bytes 2097152 | tf_op jit(solution)/shard_map/all_to_all | solution.py:188
  189.0 25.1 %all-to-all-done.2 = bf16[2,1024,1,256]{3,0,2,1:T(2,128)(2,1)S(1)} async-done(((bf16[2,1024,1,256]{3,0,2,1:T(2,128)(2,1)}), bf16[2,1024,1,256]{3,0,2,1:T(2,128)(2,1)S(1)}, u32[]{:S(2)}, u32[]{:S(2)}) %all-to-all-start.2) | async-done | bytes 1048608 | tf_op jit(solution)/shard_map/all_to_all | solution.py:188
  220.4 11.3 fusion.92
  231.7 10.6 all-gather.17.cloned.1.call-done
  242.2 11.1 fusion.91
  253.4 49.6 %all-gather.21.cloned.1.call-done = bf16[1024,4608]{1,0:T(8,128)(2,1)} async-done(((bf16[128,4608]{1,0:T(8,128)(2,1)}), bf16[1024,4608]{1,0:T(8,128)(2,1)}) %all-gather.21.cloned.1.call-update) | async-done | bytes 9437200 | tf_op jit(solution)/shard_map/all_gather | solution.py:219
  303.0 16.8 %multiply_convert_fusion = (bf16[512,4608]{1,0:T(8,128)(2,1)S(1)}, bf16[512,4608]{1,0:T(8,128)(2,1)}, bf16[512,4608]{1,0:T(8,128)(2,1)}) fusion(f32[512,4608]{1,0:T(8,128)} %fusion.91, f32[512,4608]{1,0:T(8,128)} %fusion.92, bf16[512,1024]{1,0:T(8,128)(2,1)} %bitcast.305, bf16[1024,4608]{1,0:T(8,128)(2,1)} %all-gather.21.cloned.1.call-done), kind=kOutput, calls=%fused_computation.12 | convolution fusion | flops 4867227648 | bytes 43515904 | tf_op jit(solution)/shard_map/dot_general | solution.py:56
  319.8 10.8 fusion.93
  330.7 8.1 multiply_reduce_fusion.1
  347.6 5.0 all-to-all-start.3
  352.7 11.6 convolution_dynamic-update-slice_fusion.1
  364.3 11.7 convolution_dynamic-update-slice_fusion
  383.7 5.9 fusion.54
  390.2 6.4 fusion.9
  396.5 8.9 fusion.48
  405.4 11.2 fusion.1
  418.6 3.6 fusion.58
  422.1 6.8 fusion.51
  433.4 4.2 all-to-all-start.5
  437.6 11.9 bitcast_dynamic-update-slice_fusion
  449.5 4.9 fusion.53
  455.6 4.0 fusion.52
  461.5 3.5 pad_maximum_fusion.4
  465.0 5.0 all-to-all-start.4
  485.6 9.3 all-to-all-done.4
  497.8 4.1 copy.124
  502.0 3.9 reshape.510
  509.6 3.5 convolution_dynamic-update-slice_fusion.2
  518.7 16.5 %collective-permute-done = bf16[128,4608]{1,0:T(8,128)(2,1)S(1)} collective-permute-done((bf16[128,4608]{1,0:T(8,128)(2,1)S(1)}, bf16[128,4608]{1,0:T(8,128)(2,1)S(1)}, u32[]{:S(2)}, u32[]{:S(2)}) %collective-permute-start) | collective-permute-done | bytes 1179680 | tf_op jit(solution)/shard_map/ppermute | solution.py:209
  537.9 26.5 %collective-permute-done.1 = bf16[128,4608]{1,0:T(8,128)(2,1)S(1)} collective-permute-done((bf16[128,4608]{1,0:T(8,128)(2,1)S(1)}, bf16[128,4608]{1,0:T(8,128)(2,1)S(1)}, u32[]{:S(2)}, u32[]{:S(2)}) %collective-permute-start.1) | collective-permute-done | bytes 1179680 | tf_op jit(solution)/shard_map/ppermute | solution.py:209
  567.0 26.2 %collective-permute-done.2 = bf16[128,4608]{1,0:T(8,128)(2,1)} collective-permute-done((bf16[128,4608]{1,0:T(8,128)(2,1)S(1)}, bf16[128,4608]{1,0:T(8,128)(2,1)}, u32[]{:S(2)}, u32[]{:S(2)}) %collective-permute-start.2) | collective-permute-done | bytes 1179680 | tf_op jit(solution)/shard_map/ppermute | solution.py:209
  596.1 25.9 %collective-permute-done.3 = bf16[128,4608]{1,0:T(8,128)(2,1)} collective-permute-done((bf16[128,4608]{1,0:T(8,128)(2,1)}, bf16[128,4608]{1,0:T(8,128)(2,1)}, u32[]{:S(2)}, u32[]{:S(2)}) %collective-permute-start.3) | collective-permute-done | bytes 1179680 | tf_op jit(solution)/shard_map/ppermute | solution.py:209
  643.7 489.3 %reduce-scatter.2.cloned.1.call-done = f32[32,16896]{1,0:T(8,128)} async-done(((f32[1024,16896]{1,0:T(8,128)}), f32[32,16896]{1,0:T(8,128)}) %reduce-scatter.2.cloned.1.call-update) | async-done | bytes 2162704 | tf_op jit(solution)/shard_map/reduce_scatter | solution.py:68
  1144.0 10.4 add_convert_fusion
  1159.4 44.0 %all-reduce.2 = (f32[1024]{0:T(1024)}, f32[1024]{0:T(1024)}, f32[64]{0:T(128)}, f32[64]{0:T(128)}) all-reduce(f32[1024]{0:T(1024)S(1)} %get-tuple-element.81, f32[1024]{0:T(1024)S(1)} %get-tuple-element.79, f32[64]{0:T(128)S(1)} %get-tuple-element.77, f32[64]{0:T(128)S(1)} %get-tuple-element.83), channel_id=1, replica_groups=mesh['dp'=8,'seq'=4] {'dp','seq'}, use_global_device_ids=true, to_apply=%region_16.17 | all-reduce | flops 2176 | bytes 17408 | tf_op jit(solution)/shard_map/psum | solution.py:348
  1206.6 14.4 %all_gather.43 = bf16[128,1024]{1,0:T(8,128)(2,1)S(1)} all-gather(bf16[32,1024]{1,0:T(8,128)(2,1)S(1)} %slice-done), channel_id=1, replica_groups=mesh['dp'=8,'seq'=4] {'seq'}, dimensions={0}, use_global_device_ids=true | all-gather | bytes 327680 | tf_op jit(solution)/shard_map/all_gather | solution.py:341
  1221.8 14.7 %all_gather.42 = bf16[128,2048]{1,0:T(8,128)(2,1)S(1)} all-gather(bf16[32,2048]{1,0:T(8,128)(2,1)S(1)} %slice-done.1), channel_id=1, replica_groups=mesh['dp'=8,'seq'=4] {'seq'}, dimensions={0}, use_global_device_ids=true | all-gather | bytes 655360 | tf_op jit(solution)/shard_map/all_gather | solution.py:344
  1238.3 5.2 fusion.85
  (273 shorter events, 153.2 us)
Async XLA Ops:
  7.2 28.9 %all-gather.11.cloned.1.call-start = ((), (), s32[]{:S(2)}) async-start(), calls=%async_computation.8 | async-start | bytes 1179648 | tf_op jit(solution)/shard_map/all_gather | solution.py:115
  7.9 53.6 %all-gather.9.cloned.1.call-start = ((), (), s32[]{:S(2)}) async-start(), calls=%async_computation.7 | async-start | bytes 1179648 | tf_op jit(solution)/shard_map/all_gather | solution.py:114
  8.7 82.7 %all-gather.13.cloned.1.call-start = ((), (), s32[]{:S(2)}) async-start(), calls=%async_computation.9 | async-start | bytes 2359296 | tf_op jit(solution)/shard_map/all_gather | solution.py:113
  9.4 206.0 %all-gather.15.cloned.1.call-start = ((), (), s32[]{:S(2)}) async-start(), calls=%async_computation.10 | async-start | bytes 2359296 | tf_op jit(solution)/shard_map/all_gather | solution.py:116
  10.0 210.4 %all-gather.19.cloned.1.call-start = ((), (), s32[]{:S(2)}) async-start(), calls=%async_computation.12 | async-start | bytes 10616832 | tf_op jit(solution)/shard_map/all_gather | solution.py:195
  10.6 231.7 %all-gather.17.cloned.1.call-start = ((), (), s32[]{:S(2)}) async-start(), calls=%async_computation.11 | async-start | bytes 10616832 | tf_op jit(solution)/shard_map/all_gather | solution.py:194
  11.2 291.8 %all-gather.21.cloned.1.call-start = ((), (), s32[]{:S(2)}) async-start(), calls=%async_computation.13 | async-start | bytes 10616832 | tf_op jit(solution)/shard_map/all_gather | solution.py:219
  13.3 82.1 %copy-start.21 = (bf16[2,256,1024]{2,1,0:T(8,128)(2,1)}, bf16[2,256,1024]{2,1,0:T(8,128)(2,1)S(1)}, u32[]{:S(2)}) copy-start(bf16[2,256,1024]{2,1,0:T(8,128)(2,1)S(1)} %fusion.34) | copy-start | bytes 3145732
  13.9 86.1 %copy-start.37 = (f32[512,32]{0,1:T(8,128)}, f32[512,32]{0,1:T(8,128)S(1)}, u32[]{:S(2)}) copy-start(f32[512,32]{0,1:T(8,128)S(1)} %get-tuple-element.111) | copy-start | bytes 196612
  13.9 86.1 %copy-start.39 = (f32[512,32]{0,1:T(8,128)}, f32[512,32]{0,1:T(8,128)S(1)}, u32[]{:S(2)}) copy-start(f32[512,32]{0,1:T(8,128)S(1)} %get-tuple-element.112) | copy-start | bytes 196612
  38.9 25.9 %copy-start.61 = (f32[64]{0:T(128)S(1)}, f32[64]{0:T(128)}, u32[]{:S(2)}) copy-start(f32[64]{0:T(128)} %param.39) | copy-start | bytes 772
  68.0 33.6 %all-to-all-start = ((bf16[2,256,4,256]{3,1,0,2:T(8,128)(2,1)}), bf16[2,256,4,256]{3,1,0,2:T(8,128)(2,1)S(1)}, u32[]{:S(2)}, u32[]{:S(2)}) async-start(bf16[2,256,4,256]{3,1,0,2:T(8,128)(2,1)} %pad_maximum_fusion.1), calls=%async_computation | async-start | bytes 2097152 | tf_op jit(solution)/shard_map/all_to_all | solution.py:142
  101.6 31.0 %all-to-all-start.1 = ((bf16[2,256,4,256]{1,0,3,2:T(2,128)(2,1)}), bf16[2,256,4,256]{1,0,3,2:T(2,128)(2,1)S(1)}, u32[]{:S(2)}, u32[]{:S(2)}) async-start(bf16[2,256,4,256]{1,0,3,2:T(2,128)(2,1)} %convert_element_type.176), calls=%async_computation.1 | async-start | bytes 2097152 | tf_op jit(solution)/shard_map/all_to_all | solution.py:141
  134.1 9.8 copy-start.24
  151.6 10.6 copy-start.50
  162.2 9.8 copy-start.36
  174.4 39.8 %all-to-all-start.2 = ((bf16[2,1024,1,256]{3,0,2,1:T(2,128)(2,1)}), bf16[2,1024,1,256]{3,0,2,1:T(2,128)(2,1)S(1)}, u32[]{:S(2)}, u32[]{:S(2)}) async-start(bf16[2,1024,1,256]{3,0,2,1:T(2,128)(2,1)} %pad_maximum_fusion.3), calls=%async_computation.2 | async-start | bytes 2097152 | tf_op jit(solution)/shard_map/all_to_all | solution.py:188
  319.8 10.8 copy-start.19
  319.8 10.8 copy-start.9
  347.6 31.2 %all-to-all-start.3 = ((bf16[2,256,4,256]{1,3,0,2:T(8,128)(2,1)}), bf16[2,256,4,256]{1,3,0,2:T(8,128)(2,1)}, u32[]{:S(2)}, u32[]{:S(2)}) async-start(bf16[2,256,4,256]{1,3,0,2:T(8,128)(2,1)} %copy.117), calls=%async_computation.3 | async-start | bytes 2097152 | tf_op jit(solution)/shard_map/all_to_all | solution.py:231
  383.7 12.8 %copy-start.28 = (bf16[2,1024,2,2,64]{1,4,3,2,0:T(8,128)(2,1)}, bf16[2,1024,2,2,64]{1,4,3,2,0:T(8,128)(2,1)S(1)}, u32[]{:S(2)}) copy-start(bf16[2,1024,2,2,64]{1,4,3,2,0:T(8,128)(2,1)S(1)} %reshape.504) | copy-start | bytes 3145732
  405.4 13.2 %copy-start.25 = (bf16[2,1024,2,2,64]{1,4,3,2,0:T(8,128)(2,1)S(1)}, bf16[2,1024,2,2,64]{1,4,3,2,0:T(8,128)(2,1)}, u32[]{:S(2)}) copy-start(bf16[2,1024,2,2,64]{1,4,3,2,0:T(8,128)(2,1)} %copy-done.24) | copy-start | bytes 3145732
  433.4 31.7 %all-to-all-start.5 = ((bf16[2,1024,1,256]{3,0,2,1:T(2,128)(2,1)}), bf16[2,1024,1,256]{3,0,2,1:T(2,128)(2,1)}, u32[]{:S(2)}, u32[]{:S(2)}) async-start(bf16[2,1024,1,256]{3,0,2,1:T(2,128)(2,1)} %pad_maximum_fusion.5), calls=%async_computation.5 | async-start | bytes 2097152 | tf_op jit(solution)/shard_map/all_to_all | solution.py:281
  437.6 11.9 copy-start.30
  455.6 14.7 %copy-start.27 = (bf16[64,8,4,256]{3,1,2,0:T(8,128)(2,1)S(1)}, bf16[64,8,4,256]{3,1,2,0:T(8,128)(2,1)}, u32[]{:S(2)}) copy-start(bf16[64,8,4,256]{3,1,2,0:T(8,128)(2,1)} %copy-done.26) | copy-start | bytes 3145732
  465.0 29.9 %all-to-all-start.4 = ((bf16[2,1024,1,256]{3,0,2,1:T(2,128)(2,1)}), bf16[2,1024,1,256]{3,0,2,1:T(2,128)(2,1)}, u32[]{:S(2)}, u32[]{:S(2)}) async-start(bf16[2,1024,1,256]{3,0,2,1:T(2,128)(2,1)} %pad_maximum_fusion.4), calls=%async_computation.4 | async-start | bytes 2097152 | tf_op jit(solution)/shard_map/all_to_all | solution.py:280
  470.1 662.9 %reduce-scatter.2.cloned.1.call-start = ((), (), s32[]{:S(2)}) async-start(), calls=%async_computation.14 | async-start | bytes 71368704 | tf_op jit(solution)/shard_map/reduce_scatter | solution.py:68
  473.7 9.1 copy-start.38
  473.7 9.1 copy-start.40
  475.1 9.0 copy-start.6
  475.1 9.0 copy-start.53
  517.4 720.8 %all-gather.23.cloned.1.call-start = ((), (), s32[]{:S(2)}) async-start(), calls=%async_computation.15 | async-start | bytes 4423680 | tf_op jit(solution)/shard_map/all_gather | solution.py:338
  518.7 16.5 %collective-permute-start = (bf16[128,4608]{1,0:T(8,128)(2,1)S(1)}, bf16[128,4608]{1,0:T(8,128)(2,1)S(1)}, u32[]{:S(2)}, u32[]{:S(2)}) collective-permute-start(bf16[128,4608]{1,0:T(8,128)(2,1)S(1)} %copy-done.4), channel_id=1, source_target_pairs={{0,4},{4,8},{8,12},{12,16},{16,20},{20,24},{24,28},{28,0},{1,5},{5... | collective-permute-start | bytes 3538952 | tf_op jit(solution)/shard_map/ppermute | solution.py:209
  535.2 29.1 %copy-start.13 = (bf16[128,4608]{1,0:T(8,128)(2,1)}, bf16[128,4608]{1,0:T(8,128)(2,1)S(1)}, u32[]{:S(2)}) copy-start(bf16[128,4608]{1,0:T(8,128)(2,1)S(1)} %collective-permute-done) | copy-start | bytes 3538948
  535.2 29.1 %collective-permute-start.1 = (bf16[128,4608]{1,0:T(8,128)(2,1)S(1)}, bf16[128,4608]{1,0:T(8,128)(2,1)S(1)}, u32[]{:S(2)}, u32[]{:S(2)}) collective-permute-start(bf16[128,4608]{1,0:T(8,128)(2,1)S(1)} %collective-permute-done), channel_id=1, source_target_pairs={{0,4},{4,8},{8,12},{12,16},{16,20},{20,24},{24,28},{28,0},{1,5},{5... | collective-permute-start | bytes 3538952 | tf_op jit(solution)/shard_map/ppermute | solution.py:209
  535.2 29.1 %collective-permute-start.4 = (bf16[128,4608]{1,0:T(8,128)(2,1)S(1)}, bf16[128,4608]{1,0:T(8,128)(2,1)}, u32[]{:S(2)}, u32[]{:S(2)}) collective-permute-start(bf16[128,4608]{1,0:T(8,128)(2,1)S(1)} %copy-done.4), channel_id=1, source_target_pairs={{0,28},{4,0},{8,4},{12,8},{16,12},{20,16},{24,20},{28,24},{1,29},{... | collective-permute-start | bytes 3538952 | tf_op jit(solution)/shard_map/ppermute | solution.py:211
  564.3 28.8 %collective-permute-start.2 = (bf16[128,4608]{1,0:T(8,128)(2,1)S(1)}, bf16[128,4608]{1,0:T(8,128)(2,1)}, u32[]{:S(2)}, u32[]{:S(2)}) collective-permute-start(bf16[128,4608]{1,0:T(8,128)(2,1)S(1)} %collective-permute-done.1), channel_id=1, source_target_pairs={{0,4},{4,8},{8,12},{12,16},{16,20},{20,24},{24,28},{28,0},{1,5},{5... | collective-permute-start | bytes 3538952 | tf_op jit(solution)/shard_map/ppermute | solution.py:209
  564.4 28.8 %collective-permute-start.5 = (bf16[128,4608]{1,0:T(8,128)(2,1)}, bf16[128,4608]{1,0:T(8,128)(2,1)}, u32[]{:S(2)}, u32[]{:S(2)}) collective-permute-start(bf16[128,4608]{1,0:T(8,128)(2,1)} %collective-permute-done.4), channel_id=1, source_target_pairs={{0,28},{4,0},{8,4},{12,8},{16,12},{20,16},{24,20},{28,24},{1,29},{... | collective-permute-start | bytes 3538952 | tf_op jit(solution)/shard_map/ppermute | solution.py:211
  593.2 28.8 %collective-permute-start.3 = (bf16[128,4608]{1,0:T(8,128)(2,1)}, bf16[128,4608]{1,0:T(8,128)(2,1)}, u32[]{:S(2)}, u32[]{:S(2)}) collective-permute-start(bf16[128,4608]{1,0:T(8,128)(2,1)} %collective-permute-done.2), channel_id=1, source_target_pairs={{0,4},{4,8},{8,12},{12,16},{16,20},{20,24},{24,28},{28,0},{1,5},{5... | collective-permute-start | bytes 3538952 | tf_op jit(solution)/shard_map/ppermute | solution.py:209
  593.2 33.8 %copy-start.16 = (bf16[128,4608]{1,0:T(8,128)(2,1)S(1)}, bf16[128,4608]{1,0:T(8,128)(2,1)}, u32[]{:S(2)}) copy-start(bf16[128,4608]{1,0:T(8,128)(2,1)} %copy-done.15) | copy-start | bytes 3538948
  593.2 34.9 %copy-start.14 = (bf16[128,4608]{1,0:T(8,128)(2,1)S(1)}, bf16[128,4608]{1,0:T(8,128)(2,1)}, u32[]{:S(2)}) copy-start(bf16[128,4608]{1,0:T(8,128)(2,1)} %copy-done.13) | copy-start | bytes 3538948
  593.2 41.9 %collective-permute-start.6 = (bf16[128,4608]{1,0:T(8,128)(2,1)}, bf16[128,4608]{1,0:T(8,128)(2,1)S(1)}, u32[]{:S(2)}, u32[]{:S(2)}) collective-permute-start(bf16[128,4608]{1,0:T(8,128)(2,1)} %collective-permute-done.5), channel_id=1, source_target_pairs={{0,28},{4,0},{8,4},{12,8},{16,12},{20,16},{24,20},{28,24},{1,29},{... | collective-permute-start | bytes 3538952 | tf_op jit(solution)/shard_map/ppermute | solution.py:211
  1144.0 10.4 copy-start.12
  1144.0 10.4 copy-start.23
  1144.0 11.2 copy-start.35
  1144.0 11.2 copy-start.46
  1159.4 47.2 %slice-start = ((bf16[32,16896]{1,0:T(8,128)(2,1)}), bf16[32,1024]{1,0:T(8,128)(2,1)S(1)}, s32[]{:S(2)}) async-start(bf16[32,16896]{1,0:T(8,128)(2,1)} %copy-done.20), calls=%async_computation.16 | async-start | bytes 131072 | tf_op jit(solution)/shard_map/slice | solution.py:335
  1159.4 62.5 %slice-start.1 = ((bf16[32,16896]{1,0:T(8,128)(2,1)}), bf16[32,2048]{1,0:T(8,128)(2,1)S(1)}, s32[]{:S(2)}) async-start(bf16[32,16896]{1,0:T(8,128)(2,1)} %copy-done.20), calls=%async_computation.17 | async-start | bytes 262144 | tf_op jit(solution)/shard_map/slice | solution.py:336
  (40 other events, 160.2 us)
Sparse Core Ops, SparseCore 0:
  9.9 26.1 all-gather.10
  38.0 23.4 all-gather.8
  63.5 27.8 all-gather.12
  93.1 27.8 all-gather.14
  122.8 58.8 all-gather.18
  183.4 58.8 all-gather.16
  244.1 58.8 all-gather.20
  517.6 615.3 reduce-scatter.1
  1136.9 70.6 all-gather.22
